TPU v7x, 32 devices: a whole 2x2x4 slice. The times are simulated.
32 devices in a mesh: wide: 8 (over z, y), narrow: 4 (over x, core).
Axes of the slice: x: 2, y: 2, z: 4, core: 2. Of those that a mesh axis runs over, the one named last changes fastest.
Arguments:
- fine_in: bfloat16 [32, 32, 64, 80], P(None, 'narrow', 'wide'), may hold values from -6 to 6
- voxel_mask: int32 [32, 64, 80], P('narrow', 'wide'), may hold values from 0 to 1, as said below
- timestep: int32 [1], replicated, may hold values from 0 to 999
- w_enc: bfloat16 [27, 32, 32], replicated, may hold values from -0.21875 to 0.21875
- b_enc: float32 [32], replicated, may hold values from -3 to 3
- w_down: bfloat16 [128, 256], replicated, may hold values from -0.375 to 0.375
- w_time: bfloat16 [128, 256], replicated, may hold values from -0.5 to 0.5
- w_coarse: bfloat16 [27, 128, 128], replicated, may hold values from -0.109375 to 0.109375
- b_coarse: float32 [128], replicated, may hold values from -3 to 3
- w_up: bfloat16 [32, 128], replicated, may hold values from -0.5 to 0.5
- w_dec: bfloat16 [27, 32, 64], replicated, may hold values from -0.15625 to 0.15625
- b_dec: float32 [32], replicated, may hold values from -3 to 3
Outputs:
- denoised: bfloat16 [32, 32, 64, 80], P(None, 'narrow', 'wide')
Inputs may be any that keep to these rules, and one draw needn't show every extreme that they name: `voxel_mask`: each device's tile of 8 x 8 x 80 voxels consists of aligned 8 x 8 x 8 blocks; a block is active when it holds a 1. Two tiles with the same narrow index whose wide indices differ by 4 hold at most 10 active blocks together, and some such pair holds exactly 10.
All inputs are finite; a program needn't handle non-finite values.
Results may differ from a plain program's by a relative error of at most 0.0044.
Values may be sent and summed in bfloat16 or wider, within the bound.
A program may use at most 64 MiB of HBM per device.

v0:
```python
import functools
import math

import jax
import jax.numpy as jnp
from jax import lax
from jax.experimental import pallas as pl
from jax.experimental.pallas import tpu as pltpu
from jax.sharding import PartitionSpec as P

BF = jnp.bfloat16
F32 = jnp.float32
LANES = 128
WAYS = [(1, 0), (-1, 0), (0, 1), (0, -1), (1, 1), (1, -1), (-1, 1), (-1, -1)]
NT = (((1,), (1,)), ((), ()))


def round_up(n, m):
    return -(-n // m) * m


def time_features(timestep, embed_width):
    halves = embed_width // 2
    freqs = jnp.exp(-math.log(10000.0) * jnp.arange(halves, dtype=F32) / halves)
    angles = timestep[0].astype(F32) * freqs
    return jnp.concatenate([jnp.sin(angles), jnp.cos(angles)]).astype(BF)


def silu(v):
    return v / (1.0 + jnp.exp(-v))


def edge(step, size, landing):
    if step == 0:
        return pl.ds(1, size)
    if landing:
        return pl.ds(0 if step == 1 else size + 1, 1)
    return pl.ds(size if step == 1 else 1, 1)


def fine_kernel(
    n_narrow, n_wide,
    fine_ref, mask_ref, rows_ref, cols_ref, w_enc_ref, w_down_ref, w_coarse_ref, w_up_ref, w_dec_ref,
    out_ref,
    masked, enc, coarse, lift, on_keep, mask_keep, turn, acc, k_enc, k_dec_e, k_dec_l, k_down,
    send_sem, recv_sem,
):
    chans, tx, ty, tz = fine_ref.shape
    cx, cy = tx // 2, ty // 2
    kz = coarse.shape[2]
    zl = masked.shape[3]
    cc = w_up_ref.shape[1]
    ni, wi = lax.axis_index("narrow"), lax.axis_index("wide")

    def there(dx, dy):
        ok = None
        for pos, step, size in ((ni, dx, n_narrow), (wi, dy, n_wide)):
            if step == 1:
                one = pos < size - 1
            elif step == -1:
                one = pos > 0
            else:
                continue
            ok = one if ok is None else jnp.logical_and(ok, one)
        return ok

    def copy(phase, buf, way):
        dx, dy = WAYS[way]
        sx, sy = buf.shape[0] - 2, buf.shape[1] - 2
        return pltpu.make_async_remote_copy(
            src_ref=buf.at[edge(dx, sx, False), edge(dy, sy, False)],
            dst_ref=buf.at[edge(dx, sx, True), edge(dy, sy, True)],
            send_sem=send_sem.at[phase, way],
            recv_sem=recv_sem.at[phase, way],
            device_id={"narrow": ni + dx, "wide": wi + dy},
            device_id_type=pl.DeviceIdType.MESH,
        )

    def send(phase, buf):
        for way, (dx, dy) in enumerate(WAYS):
            @pl.when(there(dx, dy))
            def _():
                copy(phase, buf, way).start()

    def arrive(phase, buf):
        for way, (dx, dy) in enumerate(WAYS):
            @pl.when(there(-dx, -dy))
            def _():
                copy(phase, buf, way).wait_recv()

    def sent(phase, buf):
        for way, (dx, dy) in enumerate(WAYS):
            @pl.when(there(dx, dy))
            def _():
                copy(phase, buf, way).wait_send()

    for buf in (masked, enc, coarse, lift):
        sx, sy = buf.shape[0], buf.shape[1]
        for at in (0, sx - 1):
            buf[at] = jnp.zeros(buf.shape[1:], BF)
        for at in (0, sy - 1):
            buf[:, at] = jnp.zeros((sx,) + buf.shape[2:], BF)

    barrier = pltpu.get_barrier_semaphore()
    for dx, dy in WAYS:
        @pl.when(there(dx, dy))
        def _():
            pl.semaphore_signal(
                barrier, inc=1, device_id={"narrow": ni + dx, "wide": wi + dy},
                device_id_type=pl.DeviceIdType.MESH,
            )

    turn[...] = jnp.zeros(turn.shape, F32)
    mask_keep[...] = jnp.zeros(mask_keep.shape, F32)
    mask_keep[:, :, 0:tz] = mask_ref[...].astype(F32)

    @pl.loop(0, tx)
    def _(x):
        tile = fine_ref[:, x].astype(F32)
        tile = jnp.where(mask_ref[x][None] > 0, tile, 0.0)
        turn[x, :, 0:tz] = tile.reshape(chans * ty, tz)
        for y in range(ty):
            masked[1 + x, 1 + y] = turn[x, pl.ds(y, chans, stride=ty), :].astype(BF)

    across = 1 + (ni > 0).astype(jnp.int32) + (ni < n_narrow - 1).astype(jnp.int32)
    along = 1 + (wi > 0).astype(jnp.int32) + (wi < n_wide - 1).astype(jnp.int32)
    pl.semaphore_wait(barrier, across * along - 1)
    send(0, masked)

    for ref in (k_enc, k_dec_e, k_dec_l):
        ref[...] = jnp.zeros(ref.shape, BF)
    m3 = 3 * chans
    for a in range(3):
        for b in range(3):
            tap = 9 * a + 3 * b
            we = w_enc_ref[tap:tap + 3].reshape(m3, chans)
            wd = w_dec_ref[tap:tap + 3].reshape(m3, 2 * chans)
            for dx in range(2):
                rows = slice(dx * m3, dx * m3 + m3)
                at = ((a + dx) * 3 + b) * chans
                k_enc[rows, at:at + chans] = we
                k_dec_e[rows, at:at + chans] = wd[:, 0:chans]
                k_dec_l[rows, at:at + chans] = wd[:, chans:]
    for a in range(2):
        for b in range(2):
            for c in range(2):
                src = (4 * a + 2 * b + c) * chans
                dst = (4 * c + 2 * a + b) * chans
                k_down[:, dst:dst + chans] = w_down_ref[:, src:src + chans]

    row = lax.broadcasted_iota(jnp.int32, (kz, zl), 0)
    lane = lax.broadcasted_iota(jnp.int32, (kz, zl), 1)
    inside = lane < tz
    even = jnp.logical_and(lane == 2 * row, inside).astype(F32)
    odd = jnp.logical_and(lane == 2 * row + 1, inside).astype(F32)
    picks = jnp.concatenate([even, odd], axis=0).astype(BF)
    spread = (even + odd).astype(BF)

    def gather_fine(buf, x2, y0):
        parts = []
        for a in range(4):
            for b in range(3):
                parts.append(jnp.concatenate([buf[2 * x2 + a, y0 + b], buf[2 * x2 + a, y0 + 1 + b]], axis=1))
        return jnp.concatenate(parts, axis=0)

    def gather_lift(x2, y0):
        parts = []
        for a in range(4):
            for b in range(3):
                xa = x2 + (a + 1) // 2
                parts.append(jnp.concatenate(
                    [lift[xa, (y0 + b + 1) // 2], lift[xa, (y0 + b + 2) // 2]], axis=1))
        return jnp.concatenate(parts, axis=0)

    def fold(part, dx, dy):
        r = part[dx * m3:(dx + 1) * m3, dy * zl:(dy + 1) * zl]
        return (pltpu.roll(r[0:chans], 1, 1) + r[chans:2 * chans]
                + pltpu.roll(r[2 * chans:], zl - 1, 1))

    arrive(0, masked)

    @pl.loop(0, cx)
    def _(x2):
        for y0 in range(0, ty, 2):
            part = jnp.dot(k_enc[...], gather_fine(masked, x2, y0), preferred_element_type=F32)
            for dx in range(2):
                for dy in range(2):
                    v = silu(fold(part, dx, dy) + cols_ref[0:chans])
                    m = mask_keep[2 * x2 + dx, y0 + dy:y0 + dy + 1, :]
                    enc[1 + 2 * x2 + dx, 1 + y0 + dy] = jnp.where(m > 0, v, 0.0).astype(BF)

    send(1, enc)

    gains, shifts, b_coarse = rows_ref[0:1], rows_ref[1:2], rows_ref[2:3]

    @pl.loop(0, cx)
    def _(x2):
        for y2 in range(cy):
            block = enc[pl.ds(1 + 2 * x2, 2), 1 + 2 * y2:3 + 2 * y2].reshape(4 * chans, zl)
            both = lax.dot_general(picks, block, NT, preferred_element_type=F32).astype(BF)
            pooled = jnp.concatenate([both[0:kz], both[kz:]], axis=1)
            lifted = lax.dot_general(pooled, k_down[...], NT, preferred_element_type=F32)
            two = mask_keep[2 * x2, 2 * y2:2 * y2 + 2] + mask_keep[2 * x2 + 1, 2 * y2:2 * y2 + 2]
            four = jnp.broadcast_to(jnp.sum(two, axis=0, keepdims=True), (cc, zl)).astype(BF)
            on = lax.dot_general(spread, four, NT, preferred_element_type=F32)
            on_keep[x2, y2] = on
            v = silu(lifted * gains + shifts)
            coarse[1 + x2, 1 + y2] = jnp.where(on > 0, v, 0.0).astype(BF)

    send(2, coarse)
    arrive(2, coarse)

    halves = 2 if cx % 2 == 0 else 1

    @pl.loop(0, cx // halves)
    def _(x2):
        x2 = x2 * halves
        taps, weights = [], []
        for a in range(3):
            for b in range(3):
                taps.append(coarse[pl.ds(x2 + a, halves), b:b + cy].reshape(halves * cy * kz, cc))
                tap = 9 * a + 3 * b
                weights.append(w_coarse_ref[tap:tap + 3].reshape(3 * cc, cc))
        r = lax.dot_general(jnp.concatenate(taps, axis=1), jnp.concatenate(weights, axis=1), NT,
                            preferred_element_type=F32)
        n = halves * cy * kz
        v = pltpu.roll(r[:, 0:cc], 1, 0) + r[:, cc:2 * cc] + pltpu.roll(r[:, 2 * cc:], n - 1, 0)
        on = on_keep[pl.ds(x2, halves)].reshape(n, cc)
        act = jnp.where(on > 0, silu(v + b_coarse), 0.0).astype(BF)
        for h in range(halves):
            for y2 in range(cy):
                at = (h * cy + y2) * kz
                up = lax.dot_general(w_up_ref[...], act[at:at + kz], NT, preferred_element_type=F32).astype(BF)
                lift[1 + x2 + h, 1 + y2] = jnp.dot(up, spread, preferred_element_type=F32).astype(BF)

    send(3, lift)
    arrive(1, enc)

    @pl.loop(0, cx)
    def _(x2):
        for y0 in range(0, ty, 2):
            acc[x2, y0 // 2] = jnp.dot(k_dec_e[...], gather_fine(enc, x2, y0), preferred_element_type=F32)

    arrive(3, lift)

    @pl.loop(0, cx)
    def _(x2):
        for y0 in range(0, ty, 2):
            part = acc[x2, y0 // 2] + jnp.dot(
                k_dec_l[...], gather_lift(x2, y0), preferred_element_type=F32)
            for dx in range(2):
                for dy in range(2):
                    v = fold(part, dx, dy) + cols_ref[chans:2 * chans]
                    turn[2 * x2 + dx, pl.ds(y0 + dy, chans, stride=ty), :] = v
        for dx in range(2):
            tile = turn[2 * x2 + dx].reshape(chans, ty, zl)[:, :, 0:tz]
            tile = jnp.where(mask_ref[2 * x2 + dx][None] > 0, tile, 0.0)
            out_ref[:, 2 * x2 + dx] = tile.astype(BF)

    for phase, buf in enumerate((masked, enc, coarse, lift)):
        sent(phase, buf)


def on_device(n_narrow, n_wide, fine_in, voxel_mask, timestep, w_enc, b_enc, w_down, w_time,
              w_coarse, b_coarse, w_up, w_dec, b_dec):
    chans, tx, ty, tz = fine_in.shape
    cc = w_down.shape[0]
    zl = round_up(tz + 1, LANES)
    kz = round_up(tz // 2 + 1, 16)
    embedded = time_features(timestep, w_time.shape[0])
    film = jnp.dot(embedded[None], w_time, preferred_element_type=F32)[0]
    rows = jnp.stack([1.0 + film[:cc], film[cc:], b_coarse])
    cols = jnp.broadcast_to(jnp.concatenate([b_enc, b_dec])[:, None], (2 * chans, zl))
    k_rows, k_cols = 6 * chans, 12 * chans
    vmem = pl.BlockSpec(memory_space=pltpu.VMEM)
    return pl.pallas_call(
        functools.partial(fine_kernel, n_narrow, n_wide),
        out_shape=jax.ShapeDtypeStruct(fine_in.shape, BF),
        in_specs=[vmem] * 9,
        out_specs=vmem,
        scratch_shapes=[
            pltpu.VMEM((tx + 2, ty + 2, chans, zl), BF),
            pltpu.VMEM((tx + 2, ty + 2, chans, zl), BF),
            pltpu.VMEM((tx // 2 + 2, ty // 2 + 2, kz, cc), BF),
            pltpu.VMEM((tx // 2 + 2, ty // 2 + 2, chans, zl), BF),
            pltpu.VMEM((tx // 2, ty // 2, kz, cc), F32),
            pltpu.VMEM((tx, ty, zl), F32),
            pltpu.VMEM((tx, chans * ty, zl), F32),
            pltpu.VMEM((tx // 2, ty // 2, k_rows, 2 * zl), F32),
            pltpu.VMEM((k_rows, k_cols), BF),
            pltpu.VMEM((k_rows, k_cols), BF),
            pltpu.VMEM((k_rows, k_cols), BF),
            pltpu.VMEM((cc, 8 * chans), BF),
            pltpu.SemaphoreType.DMA((4, len(WAYS))),
            pltpu.SemaphoreType.DMA((4, len(WAYS))),
        ],
        compiler_params=pltpu.CompilerParams(
            collective_id=0, has_side_effects=True, vmem_limit_bytes=48 * 1024 * 1024
        ),
    )(fine_in, voxel_mask, rows, cols, w_enc, w_down, w_coarse, w_up, w_dec)


def solution(mesh):
    return jax.shard_map(
        functools.partial(on_device, mesh.shape["narrow"], mesh.shape["wide"]),
        mesh=mesh,
        in_specs=(
            P(None, "narrow", "wide", None),
            P("narrow", "wide", None),
            P(), P(), P(), P(), P(), P(), P(), P(), P(), P(),
        ),
        out_specs=P(None, "narrow", "wide", None),
        check_vma=False,
    )
```

profile of v0, /device:TPU:17, one launch (start us, length us, event | category | flops | bytes accessed | tf_op | source)
XLA Modules:
  0.0 35.5 jit_solution(11896020267942229709)
XLA Ops:
  0.0 0.0 copy-start
  0.0 0.0 copy-start.5
  0.7 0.7 %pad_maximum_fusion.1 = f32[64]{0:T(128)S(1)} fusion(f32[32]{0:T(128)} %param.23, f32[32]{0:T(128)} %param.16), kind=kLoop, calls=%fused_computation.5 | loop fusion | flops 64 | bytes 512 | tf_op jit(solution)/shard_map/concatenate | solution.py:273
  1.5 0.0 copy-done
  1.5 0.0 copy-start.8
  1.5 0.2 fusion
  1.7 0.0 copy-start.6
  1.7 0.5 %copy-done.8 = f32[128]{0:T(128)S(1)} copy-done((f32[128]{0:T(128)S(1)}, f32[128]{0:T(128)}, u32[]{:S(2)}) %copy-start.8) | copy-done | bytes 536
  2.2 0.0 copy-start.7
  2.2 0.1 broadcast_in_dim.2.cols_ref
  2.3 0.0 copy-done.5
  2.3 0.2 copy-done.6
  2.5 0.4 %copy-done.7 = bf16[32,128]{1,0:T(8,128)(2,1)S(1)} copy-done((bf16[32,128]{1,0:T(8,128)(2,1)S(1)}, bf16[32,128]{1,0:T(8,128)(2,1)}, u32[]{:S(2)}) %copy-start.7) | copy-done | bytes 8216
  2.9 0.0 copy-start.1
  2.9 1.2 %copy-done.1 = bf16[27,128,128]{2,1,0:T(8,128)(2,1)S(1)} copy-done((bf16[27,128,128]{2,1,0:T(8,128)(2,1)S(1)}, bf16[27,128,128]{2,1,0:T(8,128)(2,1)}, u32[]{:S(2)}) %copy-start.1) | copy-done | bytes 884760
  4.0 0.0 copy-start.2
  4.0 1.0 %copy-done.2 = bf16[32,8,8,80]{3,2,1,0:T(8,128)(2,1)S(1)} copy-done((bf16[32,8,8,80]{3,2,1,0:T(8,128)(2,1)S(1)}, bf16[32,8,8,80]{3,2,1,0:T(8,128)(2,1)}, u32[]{:S(2)}) %copy-start.2) | copy-done | bytes 327704
  5.1 0.0 copy-start.3
  5.1 0.9 %copy-done.3 = bf16[27,32,32]{2,1,0:T(8,128)(2,1)S(1)} copy-done((bf16[27,32,32]{2,1,0:T(8,128)(2,1)S(1)}, bf16[27,32,32]{2,1,0:T(8,128)(2,1)}, u32[]{:S(2)}) %copy-start.3) | copy-done | bytes 55320
  6.0 0.0 copy-start.4
  6.0 0.9 %copy-done.4 = bf16[27,32,64]{2,1,0:T(8,128)(2,1)S(1)} copy-done((bf16[27,32,64]{2,1,0:T(8,128)(2,1)S(1)}, bf16[27,32,64]{2,1,0:T(8,128)(2,1)}, u32[]{:S(2)}) %copy-start.4) | copy-done | bytes 110616
  7.0 27.7 %shard_map.118 = bf16[32,8,8,80]{3,2,1,0:T(8,128)(2,1)S(1)} custom-call(bf16[32,8,8,80]{3,2,1,0:T(8,128)(2,1)S(1)} %copy-done.2, s32[8,8,80]{2,1,0:T(8,128)S(1)} %copy-done.6, f32[3,128]{1,0:T(4,128)S(1)} %pad_maximum_fusion.rows_ref, f32[64,128]{1,0:T(8,128)S(1)} %broadcast_in_dim.2.cols_ref, bf16[27,32,32]{2,1,0:T(8,128)(2,1)S(1)} %copy-done.3, ...), custom_call_target="tpu_custom_call" | custom-call | tf_op jit(solution)/shard_map/pallas_call | solution.py:276
  34.7 0.8 %copy.15 = bf16[32,8,8,80]{3,2,1,0:T(8,128)(2,1)} copy(bf16[32,8,8,80]{3,2,1,0:T(8,128)(2,1)S(1)} %shard_map.118) | data formatting | bytes 655360
  (3 shorter events, 0.1 us)
Async XLA Ops:
  0.0 1.5 %copy-start = (bf16[128,256]{1,0:T(8,128)(2,1)S(1)}, bf16[128,256]{1,0:T(8,128)(2,1)}, u32[]{:S(2)}) copy-start(bf16[128,256]{1,0:T(8,128)(2,1)} %param.18) | copy-start | bytes 196612
  0.0 2.2 %copy-start.5 = (bf16[128,256]{1,0:T(8,128)(2,1)S(1)}, bf16[128,256]{1,0:T(8,128)(2,1)}, u32[]{:S(2)}) copy-start(bf16[128,256]{1,0:T(8,128)(2,1)} %w_down_ref.1) | copy-start | bytes 196612
  1.5 0.7 %copy-start.8 = (f32[128]{0:T(128)S(1)}, f32[128]{0:T(128)}, u32[]{:S(2)}) copy-start(f32[128]{0:T(128)} %param.20) | copy-start | bytes 1540
  1.7 0.8 %copy-start.6 = (s32[8,8,80]{2,1,0:T(8,128)S(1)}, s32[8,8,80]{2,1,0:T(8,128)}, u32[]{:S(2)}) copy-start(s32[8,8,80]{2,1,0:T(8,128)} %mask_ref.1) | copy-start | bytes 61444
  2.2 0.7 %copy-start.7 = (bf16[32,128]{1,0:T(8,128)(2,1)S(1)}, bf16[32,128]{1,0:T(8,128)(2,1)}, u32[]{:S(2)}) copy-start(bf16[32,128]{1,0:T(8,128)(2,1)} %w_up_ref.1) | copy-start | bytes 24580
  2.9 1.2 %copy-start.1 = (bf16[27,128,128]{2,1,0:T(8,128)(2,1)S(1)}, bf16[27,128,128]{2,1,0:T(8,128)(2,1)}, u32[]{:S(2)}) copy-start(bf16[27,128,128]{2,1,0:T(8,128)(2,1)} %w_coarse_ref.1) | copy-start | bytes 2654212
  4.0 1.0 %copy-start.2 = (bf16[32,8,8,80]{3,2,1,0:T(8,128)(2,1)S(1)}, bf16[32,8,8,80]{3,2,1,0:T(8,128)(2,1)}, u32[]{:S(2)}) copy-start(bf16[32,8,8,80]{3,2,1,0:T(8,128)(2,1)} %fine_ref.1) | copy-start | bytes 983044
  5.1 0.9 %copy-start.3 = (bf16[27,32,32]{2,1,0:T(8,128)(2,1)S(1)}, bf16[27,32,32]{2,1,0:T(8,128)(2,1)}, u32[]{:S(2)}) copy-start(bf16[27,32,32]{2,1,0:T(8,128)(2,1)} %w_enc_ref.1) | copy-start | bytes 165892
  6.0 0.9 %copy-start.4 = (bf16[27,32,64]{2,1,0:T(8,128)(2,1)S(1)}, bf16[27,32,64]{2,1,0:T(8,128)(2,1)}, u32[]{:S(2)}) copy-start(bf16[27,32,64]{2,1,0:T(8,128)(2,1)} %w_dec_ref.1) | copy-start | bytes 331780
where the time goes:
time: 35.9 us; the launch traced here: 35.5 us
  Pallas kernels  27.7 us (77%)
  local copies, waits for them, and re-layouts  6.04 us (17%)
  other arithmetic  0.81 us (2%)
  between operations  0.73 us (2%)
    pallas_call x1, Pallas kernels, on_device(): pl.pallas_call(functools.partial(fine_kernel, n_narrow, n_wide), out_shap...  27.7 us
    unnamed x19, local copies, waits for them, and re-layouts  5.96 us
    concatenate x1, other arithmetic, on_device(): jnp.concatenate([b_enc, b_dec])[:, None]  0.75 us

commit v1 on v0

--- a/solution.py
+++ b/solution.py
@@ -13,17 +13,34 @@
 LANES = 128
 WAYS = [(1, 0), (-1, 0), (0, 1), (0, -1), (1, 1), (1, -1), (-1, 1), (-1, -1)]
 NT = (((1,), (1,)), ((), ()))
+TN = (((0,), (0,)), ((), ()))
 
 
 def round_up(n, m):
     return -(-n // m) * m
 
 
-def time_features(timestep, embed_width):
-    halves = embed_width // 2
-    freqs = jnp.exp(-math.log(10000.0) * jnp.arange(halves, dtype=F32) / halves)
-    angles = timestep[0].astype(F32) * freqs
-    return jnp.concatenate([jnp.sin(angles), jnp.cos(angles)]).astype(BF)
+def reduced(angle):
+    turns = jnp.floor(angle * (0.5 / math.pi) + 0.5)
+    r = angle - turns * 6.28125
+    r = r - turns * 0.0019350051879882812
+    return r - turns * 3.019916037e-07
+
+
+def series(square, first):
+    total = jnp.zeros_like(square)
+    for power in range(first + 20, first - 1, -2):
+        total = total * square + (-1.0) ** (power // 2) / math.factorial(power)
+    return total
+
+
+def features(step_ref, width):
+    halves = width // 2
+    at = lax.broadcasted_iota(jnp.int32, (8, width), 1)
+    k = jnp.where(at < halves, at, at - halves).astype(F32)
+    r = reduced(step_ref[0].astype(F32) * jnp.exp(-math.log(10000.0) * k / halves))
+    q = r * r
+    return jnp.where(at < halves, r * series(q, 1), series(q, 0)).astype(BF)
 
 
 def silu(v):
@@ -40,11 +57,18 @@
 
 def fine_kernel(
     n_narrow, n_wide,
-    fine_ref, mask_ref, rows_ref, cols_ref, w_enc_ref, w_down_ref, w_coarse_ref, w_up_ref, w_dec_ref,
-    out_ref,
-    masked, enc, coarse, lift, on_keep, mask_keep, turn, acc, k_enc, k_dec_e, k_dec_l, k_down,
-    send_sem, recv_sem,
+    step_ref, *refs
 ):
+    inputs, refs = refs[:11], refs[11:]
+    out_ref, refs = refs[0], refs[1:]
+    local, refs = refs[:11], refs[11:]
+    loads = [pltpu.make_async_copy(a, b, refs[-1].at[i]) for i, (a, b) in enumerate(zip(inputs, local))]
+    for load in loads:
+        load.start()
+    (fine_ref, mask_ref, w_enc_ref, w_down_ref, w_dec_ref, w_time_ref, b_enc_ref, b_dec_ref,
+     b_coarse_ref, w_up_ref, w_coarse_ref) = local
+    (masked, enc, coarse, lift, flat, y_out, side_x, side_y, on_keep, mask_keep, turn, acc, k_enc, k_dec_e, k_dec_l, k_down,
+     send_sem, recv_sem, _) = refs
     chans, tx, ty, tz = fine_ref.shape
     cx, cy = tx // 2, ty // 2
     kz = coarse.shape[2]
@@ -67,9 +91,15 @@
     def copy(phase, buf, way):
         dx, dy = WAYS[way]
         sx, sy = buf.shape[0] - 2, buf.shape[1] - 2
+        src = buf.at[edge(dx, sx, False), edge(dy, sy, False)]
+        dst = buf.at[edge(dx, sx, True), edge(dy, sy, True)]
+        if phase == 3 and dy == 0:
+            src, dst = flat.at[cx - 1 if dx == 1 else 0], side_x.at[0 if dx == 1 else 1]
+        elif phase == 3 and dx == 0:
+            src, dst = y_out.at[1 if dy == 1 else 0], side_y.at[0 if dy == 1 else 1]
         return pltpu.make_async_remote_copy(
-            src_ref=buf.at[edge(dx, sx, False), edge(dy, sy, False)],
-            dst_ref=buf.at[edge(dx, sx, True), edge(dy, sy, True)],
+            src_ref=src,
+            dst_ref=dst,
             send_sem=send_sem.at[phase, way],
             recv_sem=recv_sem.at[phase, way],
             device_id={"narrow": ni + dx, "wide": wi + dy},
@@ -94,12 +124,18 @@
             def _():
                 copy(phase, buf, way).wait_send()
 
-    for buf in (masked, enc, coarse, lift):
+    for buf in (masked, enc, coarse):
         sx, sy = buf.shape[0], buf.shape[1]
         for at in (0, sx - 1):
             buf[at] = jnp.zeros(buf.shape[1:], BF)
         for at in (0, sy - 1):
             buf[:, at] = jnp.zeros((sx,) + buf.shape[2:], BF)
+
+    for buf in (side_x, side_y):
+        buf[...] = jnp.zeros(buf.shape, BF)
+    for at_x in (0, cx + 1):
+        for at_y in (0, cy + 1):
+            lift[at_x, at_y] = jnp.zeros(lift.shape[2:], BF)
 
     barrier = pltpu.get_barrier_semaphore()
     for dx, dy in WAYS:
@@ -111,6 +147,8 @@
             )
 
     turn[...] = jnp.zeros(turn.shape, F32)
+    loads[0].wait()
+    loads[1].wait()
     mask_keep[...] = jnp.zeros(mask_keep.shape, F32)
     mask_keep[:, :, 0:tz] = mask_ref[...].astype(F32)
 
@@ -126,6 +164,8 @@
     along = 1 + (wi > 0).astype(jnp.int32) + (wi < n_wide - 1).astype(jnp.int32)
     pl.semaphore_wait(barrier, across * along - 1)
     send(0, masked)
+    for load in loads[2:10]:
+        load.wait()
 
     for ref in (k_enc, k_dec_e, k_dec_l):
         ref[...] = jnp.zeros(ref.shape, BF)
@@ -156,6 +196,15 @@
     picks = jnp.concatenate([even, odd], axis=0).astype(BF)
     spread = (even + odd).astype(BF)
 
+    eye = (lax.broadcasted_iota(jnp.int32, (chans, chans), 0)
+           == lax.broadcasted_iota(jnp.int32, (chans, chans), 1))
+
+    def column(ref):
+        return jnp.broadcast_to(
+            jnp.sum(jnp.where(eye, ref[...], 0.0), axis=1, keepdims=True), (chans, zl))
+
+    b_enc, b_dec = column(b_enc_ref), column(b_dec_ref)
+
     def gather_fine(buf, x2, y0):
         parts = []
         for a in range(4):
@@ -185,13 +234,13 @@
             part = jnp.dot(k_enc[...], gather_fine(masked, x2, y0), preferred_element_type=F32)
             for dx in range(2):
                 for dy in range(2):
-                    v = silu(fold(part, dx, dy) + cols_ref[0:chans])
+                    v = silu(fold(part, dx, dy) + b_enc)
                     m = mask_keep[2 * x2 + dx, y0 + dy:y0 + dy + 1, :]
                     enc[1 + 2 * x2 + dx, 1 + y0 + dy] = jnp.where(m > 0, v, 0.0).astype(BF)
 
-    send(1, enc)
-
-    gains, shifts, b_coarse = rows_ref[0:1], rows_ref[1:2], rows_ref[2:3]
+    film = jnp.dot(features(step_ref, w_time_ref.shape[0]), w_time_ref[...], preferred_element_type=F32)
+    gains, shifts = 1.0 + film[0:1, 0:cc], film[0:1, cc:]
+    b_coarse = b_coarse_ref[...]
 
     @pl.loop(0, cx)
     def _(x2):
@@ -208,7 +257,9 @@
             coarse[1 + x2, 1 + y2] = jnp.where(on > 0, v, 0.0).astype(BF)
 
     send(2, coarse)
+    loads[10].wait()
     arrive(2, coarse)
+    send(1, enc)
 
     halves = 2 if cx % 2 == 0 else 1
 
@@ -227,12 +278,20 @@
         v = pltpu.roll(r[:, 0:cc], 1, 0) + r[:, cc:2 * cc] + pltpu.roll(r[:, 2 * cc:], n - 1, 0)
         on = on_keep[pl.ds(x2, halves)].reshape(n, cc)
         act = jnp.where(on > 0, silu(v + b_coarse), 0.0).astype(BF)
+        up = lax.dot_general(act, w_up_ref[...], NT, preferred_element_type=F32).astype(BF)
         for h in range(halves):
             for y2 in range(cy):
                 at = (h * cy + y2) * kz
-                up = lax.dot_general(w_up_ref[...], act[at:at + kz], NT, preferred_element_type=F32).astype(BF)
-                lift[1 + x2 + h, 1 + y2] = jnp.dot(up, spread, preferred_element_type=F32).astype(BF)
-
+                flat[x2 + h, :, y2 * chans:(y2 + 1) * chans] = up[at:at + kz]
+
+    def raise_z(columns, count):
+        wide = lax.dot_general(columns, spread, TN, preferred_element_type=F32)
+        return wide.astype(BF).reshape(count, chans, zl)
+
+    for x2 in range(cx):
+        for at, y2 in enumerate((0, cy - 1)):
+            y_out[at, :, x2 * chans:(x2 + 1) * chans] = flat[x2, :, y2 * chans:(y2 + 1) * chans]
+        lift[1 + x2, 1:1 + cy] = raise_z(flat[x2], cy)
     send(3, lift)
     arrive(1, enc)
 
@@ -242,6 +301,10 @@
             acc[x2, y0 // 2] = jnp.dot(k_dec_e[...], gather_fine(enc, x2, y0), preferred_element_type=F32)
 
     arrive(3, lift)
+    for at, edge_at in enumerate((0, cx + 1)):
+        lift[edge_at, 1:1 + cy] = raise_z(side_x[at], cy)
+    for at, edge_at in enumerate((0, cy + 1)):
+        lift[1:1 + cx, edge_at] = raise_z(side_y[at], cx)
 
     @pl.loop(0, cx)
     def _(x2):
@@ -250,7 +313,7 @@
                 k_dec_l[...], gather_lift(x2, y0), preferred_element_type=F32)
             for dx in range(2):
                 for dy in range(2):
-                    v = fold(part, dx, dy) + cols_ref[chans:2 * chans]
+                    v = fold(part, dx, dy) + b_dec
                     turn[2 * x2 + dx, pl.ds(y0 + dy, chans, stride=ty), :] = v
         for dx in range(2):
             tile = turn[2 * x2 + dx].reshape(chans, ty, zl)[:, :, 0:tz]
@@ -267,22 +330,25 @@
     cc = w_down.shape[0]
     zl = round_up(tz + 1, LANES)
     kz = round_up(tz // 2 + 1, 16)
-    embedded = time_features(timestep, w_time.shape[0])
-    film = jnp.dot(embedded[None], w_time, preferred_element_type=F32)[0]
-    rows = jnp.stack([1.0 + film[:cc], film[cc:], b_coarse])
-    cols = jnp.broadcast_to(jnp.concatenate([b_enc, b_dec])[:, None], (2 * chans, zl))
+    inputs = (fine_in, voxel_mask, w_enc, w_down, w_dec, w_time, b_enc[None], b_dec[None],
+              b_coarse[None], w_up, w_coarse)
     k_rows, k_cols = 6 * chans, 12 * chans
     vmem = pl.BlockSpec(memory_space=pltpu.VMEM)
     return pl.pallas_call(
         functools.partial(fine_kernel, n_narrow, n_wide),
         out_shape=jax.ShapeDtypeStruct(fine_in.shape, BF),
-        in_specs=[vmem] * 9,
+        in_specs=[pl.BlockSpec(memory_space=pltpu.SMEM)]
+        + [pl.BlockSpec(memory_space=pltpu.HBM)] * len(inputs),
         out_specs=vmem,
-        scratch_shapes=[
+        scratch_shapes=[pltpu.VMEM(a.shape, a.dtype) for a in inputs] + [
             pltpu.VMEM((tx + 2, ty + 2, chans, zl), BF),
             pltpu.VMEM((tx + 2, ty + 2, chans, zl), BF),
             pltpu.VMEM((tx // 2 + 2, ty // 2 + 2, kz, cc), BF),
             pltpu.VMEM((tx // 2 + 2, ty // 2 + 2, chans, zl), BF),
+            pltpu.VMEM((tx // 2, kz, ty // 2 * chans), BF),
+            pltpu.VMEM((2, kz, tx // 2 * chans), BF),
+            pltpu.VMEM((2, kz, ty // 2 * chans), BF),
+            pltpu.VMEM((2, kz, tx // 2 * chans), BF),
             pltpu.VMEM((tx // 2, ty // 2, kz, cc), F32),
             pltpu.VMEM((tx, ty, zl), F32),
             pltpu.VMEM((tx, chans * ty, zl), F32),
@@ -293,11 +359,12 @@
             pltpu.VMEM((cc, 8 * chans), BF),
             pltpu.SemaphoreType.DMA((4, len(WAYS))),
             pltpu.SemaphoreType.DMA((4, len(WAYS))),
+            pltpu.SemaphoreType.DMA((len(inputs),)),
         ],
         compiler_params=pltpu.CompilerParams(
             collective_id=0, has_side_effects=True, vmem_limit_bytes=48 * 1024 * 1024
         ),
-    )(fine_in, voxel_mask, rows, cols, w_enc, w_down, w_coarse, w_up, w_dec)
+    )(timestep, *inputs)
 
 
 def solution(mesh):

time: 35.9 us -> 39 us (1.086)
  local copies, waits for them, and re-layouts: 6.04 us -> 8.67 us
  Pallas kernels: 27.7 us -> 29.1 us
  other arithmetic: 0.81 us -> 0 us
    unnamed x19 -> x23, local copies, waits for them, and re-layouts: 5.96 us -> 8.67 us
    pallas_call x1, Pallas kernels: 27.7 us -> 29.1 us  [on_device(): pl.pallas_call(functools.partial(fine_kernel, n_narrow, n_wide), out_shap...]
    concatenate x1 -> x0, other arithmetic: 0.75 us -> none  [on_device(): jnp.concatenate([b_enc, b_dec])[:, None]]
where the time goes in v1:
time: 39 us; the launch traced here: 38.5 us
  Pallas kernels  29.1 us (75%)
  local copies, waits for them, and re-layouts  8.67 us (22%)
  between operations  0.69 us (2%)
    pallas_call x1, Pallas kernels, on_device(): pl.pallas_call(functools.partial(fine_kernel, n_narrow, n_wide), out_shap...  29.1 us
    unnamed x23, local copies, waits for them, and re-layouts  8.67 us

profile of v1, /device:TPU:17, one launch (start us, length us, event | category | flops | bytes accessed | tf_op | source)
XLA Modules:
  0.0 38.5 jit_solution(1868738945412799735)
XLA Ops:
  0.7 0.0 copy-start.8
  0.7 0.0 copy-start.9
  0.7 0.0 copy-start.10
  0.7 0.6 %copy-done.8 = f32[32]{0:T(128)S(1)} copy-done((f32[32]{0:T(128)S(1)}, f32[32]{0:T(128)}, u32[]{:S(2)}) %copy-start.8) | copy-done | bytes 152
  1.3 0.0 copy-done.9
  1.3 0.0 copy-done.10
  1.3 0.0 copy-start
  1.3 1.2 %copy-done = bf16[27,128,128]{2,1,0:T(8,128)(2,1)S(1)} copy-done((bf16[27,128,128]{2,1,0:T(8,128)(2,1)S(1)}, bf16[27,128,128]{2,1,0:T(8,128)(2,1)}, u32[]{:S(2)}) %copy-start) | copy-done | bytes 884760
  2.5 0.0 copy-start.1
  2.5 1.0 %copy-done.1 = bf16[32,8,8,80]{3,2,1,0:T(8,128)(2,1)S(1)} copy-done((bf16[32,8,8,80]{3,2,1,0:T(8,128)(2,1)S(1)}, bf16[32,8,8,80]{3,2,1,0:T(8,128)(2,1)}, u32[]{:S(2)}) %copy-start.1) | copy-done | bytes 327704
  3.6 0.0 copy-start.2
  3.6 0.9 %copy-done.2 = bf16[27,32,32]{2,1,0:T(8,128)(2,1)S(1)} copy-done((bf16[27,32,32]{2,1,0:T(8,128)(2,1)S(1)}, bf16[27,32,32]{2,1,0:T(8,128)(2,1)}, u32[]{:S(2)}) %copy-start.2) | copy-done | bytes 55320
  4.5 0.0 copy-start.3
  4.5 0.9 %copy-done.3 = bf16[27,32,64]{2,1,0:T(8,128)(2,1)S(1)} copy-done((bf16[27,32,64]{2,1,0:T(8,128)(2,1)S(1)}, bf16[27,32,64]{2,1,0:T(8,128)(2,1)}, u32[]{:S(2)}) %copy-start.3) | copy-done | bytes 110616
  5.4 0.0 copy-start.4
  5.4 0.8 %copy-done.4 = bf16[128,256]{1,0:T(8,128)(2,1)S(1)} copy-done((bf16[128,256]{1,0:T(8,128)(2,1)S(1)}, bf16[128,256]{1,0:T(8,128)(2,1)}, u32[]{:S(2)}) %copy-start.4) | copy-done | bytes 65560
  6.3 0.0 copy-start.5
  6.3 0.8 %copy-done.5 = bf16[128,256]{1,0:T(8,128)(2,1)S(1)} copy-done((bf16[128,256]{1,0:T(8,128)(2,1)S(1)}, bf16[128,256]{1,0:T(8,128)(2,1)}, u32[]{:S(2)}) %copy-start.5) | copy-done | bytes 65560
  7.1 0.0 copy-start.6
  7.1 0.8 %copy-done.6 = s32[8,8,80]{2,1,0:T(8,128)S(1)} copy-done((s32[8,8,80]{2,1,0:T(8,128)S(1)}, s32[8,8,80]{2,1,0:T(8,128)}, u32[]{:S(2)}) %copy-start.6) | copy-done | bytes 20504
  7.9 0.0 copy-start.7
  7.9 0.7 %copy-done.7 = bf16[32,128]{1,0:T(8,128)(2,1)S(1)} copy-done((bf16[32,128]{1,0:T(8,128)(2,1)S(1)}, bf16[32,128]{1,0:T(8,128)(2,1)}, u32[]{:S(2)}) %copy-start.7) | copy-done | bytes 8216
  8.6 29.1 %shard_map.118 = bf16[32,8,8,80]{3,2,1,0:T(8,128)(2,1)S(1)} custom-call(s32[1]{0:T(128)S(6)} %copy.14.step_ref, bf16[32,8,8,80]{3,2,1,0:T(8,128)(2,1)S(1)} %copy-done.1, s32[8,8,80]{2,1,0:T(8,128)S(1)} %copy-done.6, bf16[27,32,32]{2,1,0:T(8,128)(2,1)S(1)} %copy-done.2, bf16[128,256]{1,0:T(8,128)(2,1)S(1)} %copy-done.4, bf16[27,32,64]{2,1,0:T(8,128)(2,1)S(1)} %copy-done.3, ...), custom_call_target="tpu_custom_call" | custom-call | tf_op jit(solution)/shard_map/pallas_call | solution.py:337
  37.7 0.8 %copy.15 = bf16[32,8,8,80]{3,2,1,0:T(8,128)(2,1)} copy(bf16[32,8,8,80]{3,2,1,0:T(8,128)(2,1)S(1)} %shard_map.118) | data formatting | bytes 655360
Async XLA Ops:
  0.7 0.7 %copy-start.8 = (f32[32]{0:T(128)S(1)}, f32[32]{0:T(128)}, u32[]{:S(2)}) copy-start(f32[32]{0:T(128)} %param.16) | copy-start | bytes 388
  0.7 0.7 %copy-start.9 = (f32[32]{0:T(128)S(1)}, f32[32]{0:T(128)}, u32[]{:S(2)}) copy-start(f32[32]{0:T(128)} %param.23) | copy-start | bytes 388
  0.7 0.7 %copy-start.10 = (f32[128]{0:T(128)S(1)}, f32[128]{0:T(128)}, u32[]{:S(2)}) copy-start(f32[128]{0:T(128)} %param.20) | copy-start | bytes 1540
  1.3 1.2 %copy-start = (bf16[27,128,128]{2,1,0:T(8,128)(2,1)S(1)}, bf16[27,128,128]{2,1,0:T(8,128)(2,1)}, u32[]{:S(2)}) copy-start(bf16[27,128,128]{2,1,0:T(8,128)(2,1)} %refs_10_.1) | copy-start | bytes 2654212
  2.5 1.0 %copy-start.1 = (bf16[32,8,8,80]{3,2,1,0:T(8,128)(2,1)S(1)}, bf16[32,8,8,80]{3,2,1,0:T(8,128)(2,1)}, u32[]{:S(2)}) copy-start(bf16[32,8,8,80]{3,2,1,0:T(8,128)(2,1)} %refs_0_.1) | copy-start | bytes 983044
  3.6 0.9 %copy-start.2 = (bf16[27,32,32]{2,1,0:T(8,128)(2,1)S(1)}, bf16[27,32,32]{2,1,0:T(8,128)(2,1)}, u32[]{:S(2)}) copy-start(bf16[27,32,32]{2,1,0:T(8,128)(2,1)} %refs_2_.1) | copy-start | bytes 165892
  4.5 0.9 %copy-start.3 = (bf16[27,32,64]{2,1,0:T(8,128)(2,1)S(1)}, bf16[27,32,64]{2,1,0:T(8,128)(2,1)}, u32[]{:S(2)}) copy-start(bf16[27,32,64]{2,1,0:T(8,128)(2,1)} %refs_4_.1) | copy-start | bytes 331780
  5.4 0.8 %copy-start.4 = (bf16[128,256]{1,0:T(8,128)(2,1)S(1)}, bf16[128,256]{1,0:T(8,128)(2,1)}, u32[]{:S(2)}) copy-start(bf16[128,256]{1,0:T(8,128)(2,1)} %refs_3_.1) | copy-start | bytes 196612
  6.3 0.8 %copy-start.5 = (bf16[128,256]{1,0:T(8,128)(2,1)S(1)}, bf16[128,256]{1,0:T(8,128)(2,1)}, u32[]{:S(2)}) copy-start(bf16[128,256]{1,0:T(8,128)(2,1)} %refs_5_.1) | copy-start | bytes 196612
  7.1 0.8 %copy-start.6 = (s32[8,8,80]{2,1,0:T(8,128)S(1)}, s32[8,8,80]{2,1,0:T(8,128)}, u32[]{:S(2)}) copy-start(s32[8,8,80]{2,1,0:T(8,128)} %refs_1_.1) | copy-start | bytes 61444
  7.9 0.7 %copy-start.7 = (bf16[32,128]{1,0:T(8,128)(2,1)S(1)}, bf16[32,128]{1,0:T(8,128)(2,1)}, u32[]{:S(2)}) copy-start(bf16[32,128]{1,0:T(8,128)(2,1)} %refs_9_.1) | copy-start | bytes 24580

commit v2 on v1

--- a/solution.py
+++ b/solution.py
@@ -226,17 +226,37 @@
         return (pltpu.roll(r[0:chans], 1, 1) + r[chans:2 * chans]
                 + pltpu.roll(r[2 * chans:], zl - 1, 1))
 
+    def inner(work):
+        @pl.loop(1, cx - 1)
+        def _(x2):
+            for y0 in range(2, ty - 2, 2):
+                work(x2, y0)
+
+    def outer(work):
+        @pl.loop(1, cx - 1)
+        def _(x2):
+            for y0 in (0, ty - 2):
+                work(x2, y0)
+
+        @pl.loop(0, 2)
+        def _(end):
+            for y0 in range(0, ty, 2):
+                work(end * (cx - 1), y0)
+
+    def encode(x2, y0):
+        part = jnp.dot(k_enc[...], gather_fine(masked, x2, y0), preferred_element_type=F32)
+        for dx in range(2):
+            for dy in range(2):
+                v = silu(fold(part, dx, dy) + b_enc)
+                m = mask_keep[2 * x2 + dx, y0 + dy:y0 + dy + 1, :]
+                enc[1 + 2 * x2 + dx, 1 + y0 + dy] = jnp.where(m > 0, v, 0.0).astype(BF)
+
+    def decode_enc(x2, y0):
+        acc[x2, y0 // 2] = jnp.dot(k_dec_e[...], gather_fine(enc, x2, y0), preferred_element_type=F32)
+
+    inner(encode)
     arrive(0, masked)
-
-    @pl.loop(0, cx)
-    def _(x2):
-        for y0 in range(0, ty, 2):
-            part = jnp.dot(k_enc[...], gather_fine(masked, x2, y0), preferred_element_type=F32)
-            for dx in range(2):
-                for dy in range(2):
-                    v = silu(fold(part, dx, dy) + b_enc)
-                    m = mask_keep[2 * x2 + dx, y0 + dy:y0 + dy + 1, :]
-                    enc[1 + 2 * x2 + dx, 1 + y0 + dy] = jnp.where(m > 0, v, 0.0).astype(BF)
+    outer(encode)
 
     film = jnp.dot(features(step_ref, w_time_ref.shape[0]), w_time_ref[...], preferred_element_type=F32)
     gains, shifts = 1.0 + film[0:1, 0:cc], film[0:1, cc:]
@@ -257,6 +277,7 @@
             coarse[1 + x2, 1 + y2] = jnp.where(on > 0, v, 0.0).astype(BF)
 
     send(2, coarse)
+    inner(decode_enc)
     loads[10].wait()
     arrive(2, coarse)
     send(1, enc)
@@ -294,11 +315,7 @@
         lift[1 + x2, 1:1 + cy] = raise_z(flat[x2], cy)
     send(3, lift)
     arrive(1, enc)
-
-    @pl.loop(0, cx)
-    def _(x2):
-        for y0 in range(0, ty, 2):
-            acc[x2, y0 // 2] = jnp.dot(k_dec_e[...], gather_fine(enc, x2, y0), preferred_element_type=F32)
+    outer(decode_enc)
 
     arrive(3, lift)
     for at, edge_at in enumerate((0, cx + 1)):
@@ -362,7 +379,7 @@
             pltpu.SemaphoreType.DMA((len(inputs),)),
         ],
         compiler_params=pltpu.CompilerParams(
-            collective_id=0, has_side_effects=True, vmem_limit_bytes=48 * 1024 * 1024
+            collective_id=0, has_side_effects=True, vmem_limit_bytes=63 * 1024 * 1024
         ),
     )(timestep, *inputs)
 

time: 39 us -> 31.2 us (0.80)
  local copies, waits for them, and re-layouts: 8.67 us -> 1.87 us
  Pallas kernels: 29.1 us -> 28.5 us
    unnamed x23 -> x1, local copies, waits for them, and re-layouts: 8.67 us -> 1.87 us
    pallas_call x1, Pallas kernels: 29.1 us -> 28.5 us  [on_device(): pl.pallas_call(functools.partial(fine_kernel, n_narrow, n_wide), out_shap...]
where the time goes in v2:
time: 31.2 us; the launch traced here: 31.1 us
  Pallas kernels  28.5 us (91%)
  local copies, waits for them, and re-layouts  1.87 us (6%)
  between operations  0.66 us (2%)
    pallas_call x1, Pallas kernels, on_device(): pl.pallas_call(functools.partial(fine_kernel, n_narrow, n_wide), out_shap...  28.5 us
    unnamed x1, local copies, waits for them, and re-layouts  1.87 us

profile of v2, /device:TPU:17, one launch (start us, length us, event | category | flops | bytes accessed | tf_op | source)
XLA Modules:
  0.0 31.1 jit_solution(9189836168377537570)
XLA Ops:
  0.7 28.5 %shard_map.118 = bf16[32,8,8,80]{3,2,1,0:T(8,128)(2,1)} custom-call(s32[1]{0:T(128)S(6)} %copy.14.step_ref, bf16[32,8,8,80]{3,2,1,0:T(8,128)(2,1)} %refs_0_.1, s32[8,8,80]{2,1,0:T(8,128)} %refs_1_.1, bf16[27,32,32]{2,1,0:T(8,128)(2,1)} %refs_2_.1, bf16[128,256]{1,0:T(8,128)(2,1)} %refs_3_.1, bf16[27,32,64]{2,1,0:T(8,128)(2,1)} %refs_4_.1, ...), custom_call_target="tpu_custom_call" | custom-call | tf_op jit(solution)/shard_map/pallas_call | solution.py:354
  29.2 1.9 %copy.15 = bf16[32,8,8,80]{3,2,1,0:T(8,128)(2,1)} copy(bf16[32,8,8,80]{3,2,1,0:T(8,128)(2,1)} %shard_map.118) | data formatting | bytes 655360

commit v3 on v2

--- a/solution.py
+++ b/solution.py
@@ -282,7 +282,7 @@
     arrive(2, coarse)
     send(1, enc)
 
-    halves = 2 if cx % 2 == 0 else 1
+    halves = cx
 
     @pl.loop(0, cx // halves)
     def _(x2):
@@ -353,7 +353,7 @@
     vmem = pl.BlockSpec(memory_space=pltpu.VMEM)
     return pl.pallas_call(
         functools.partial(fine_kernel, n_narrow, n_wide),
-        out_shape=jax.ShapeDtypeStruct(fine_in.shape, BF),
+        out_shape=pltpu.VMEM(fine_in.shape, BF),
         in_specs=[pl.BlockSpec(memory_space=pltpu.SMEM)]
         + [pl.BlockSpec(memory_space=pltpu.HBM)] * len(inputs),
         out_specs=vmem,

time: 31.2 us -> 29.4 us (0.942)
  local copies, waits for them, and re-layouts: 1.87 us -> 0.8 us
  Pallas kernels: 28.5 us -> 27.7 us
    unnamed x1, local copies, waits for them, and re-layouts: 1.87 us -> 0.8 us
    pallas_call x1, Pallas kernels: 28.5 us -> 27.7 us  [on_device(): pl.pallas_call(functools.partial(fine_kernel, n_narrow, n_wide), out_shap...]
where the time goes in v3:
time: 29.4 us; the launch traced here: 29.2 us
  Pallas kernels  27.7 us (94%)
  local copies, waits for them, and re-layouts  0.8 us (3%)
  between operations  0.66 us (2%)
    pallas_call x1, Pallas kernels, on_device(): pl.pallas_call(functools.partial(fine_kernel, n_narrow, n_wide), out_shap...  27.7 us
    unnamed x1, local copies, waits for them, and re-layouts  0.8 us

profile of v3, /device:TPU:17, one launch (start us, length us, event | category | flops | bytes accessed | tf_op | source)
XLA Modules:
  0.0 29.2 jit_solution(17259676176004599538)
XLA Ops:
  0.7 27.7 %shard_map.118 = bf16[32,8,8,80]{3,2,1,0:T(8,128)(2,1)S(1)} custom-call(s32[1]{0:T(128)S(6)} %copy.15.step_ref, bf16[32,8,8,80]{3,2,1,0:T(8,128)(2,1)} %refs_0_.1, s32[8,8,80]{2,1,0:T(8,128)} %refs_1_.1, bf16[27,32,32]{2,1,0:T(8,128)(2,1)} %refs_2_.1, bf16[128,256]{1,0:T(8,128)(2,1)} %refs_3_.1, bf16[27,32,64]{2,1,0:T(8,128)(2,1)} %refs_4_.1, ...), custom_call_target="tpu_custom_call" | custom-call | tf_op jit(solution)/shard_map/pallas_call | solution.py:354
  28.4 0.8 %copy.14 = bf16[32,8,8,80]{3,2,1,0:T(8,128)(2,1)} copy(bf16[32,8,8,80]{3,2,1,0:T(8,128)(2,1)S(1)} %shard_map.118) | data formatting | bytes 655360
